TPU v7x, 32 devices: a whole 2x2x4 slice. The times are simulated.
32 devices in a mesh: basin: 2 (over x), pair: 8 (over z, y), row: 2 (over core).
Axes of the slice: x: 2, y: 2, z: 4, core: 2. Of those that a mesh axis runs over, the one named last changes fastest.
Arguments:
- snapshots: float32 [8192, 4096], P(('basin', 'row'), 'pair'), parts along dimension 0, may hold values from -60 to 60, as said below
- plan: int32 [4, 16], replicated, may hold values from 0 to 15, as said below
Outputs:
- rotated: float32 [8192, 4096], P(('basin', 'row'), 'pair'), parts along dimension 0
There are 2 independent parts, one for each index of `basin`. A program takes and returns all parts, laid end to end along the dimension named above; an argument that names none is the same for every part. Nothing has to cross between parts.
Inputs may be any that keep to these rules, and one draw needn't show every extreme that they name: `plan`: each row of the table is a permutation of the 16 slots. Slots 2d and 2d + 1 lie on the d-th index of pair; in every round each index sends one of its two blocks to index d + 1 and the other to index d - 1 (both modulo 8). `snapshots`: real values.
All inputs are finite; a program needn't handle non-finite values.
Results may differ from a plain program's by a relative error of at most 0.0003.
Values sent between devices are 32-bit elements; how exact they have to be, the bound alone decides.
No kernel may reach another device: no remote copies, remote signals or barrier semaphores. Data moves between devices by JAX's collectives and lax.ppermute only.
A program may use at most 64 MiB of HBM per device.

v0:
```python
import functools

import jax
import jax.numpy as jnp
from jax import lax
from jax.experimental import pallas as pl
from jax.experimental.pallas import tpu as pltpu
from jax.sharding import PartitionSpec as P

NS_ITERS = 6
EPSILON = 1e-06
BLOCK = 256
PIECES = (1, 3, 3, 1)
PARAMS = pltpu.CompilerParams(vmem_limit_bytes=32 * 1024 * 1024)


def shift(value, axis, by):
    size = lax.axis_size(axis)
    return lax.ppermute(value, axis, [(i, (i + by) % size) for i in range(size)])


def split(value):
    high = value.astype(jnp.bfloat16)
    return high, (value - high.astype(jnp.float32)).astype(jnp.bfloat16)


def dot(left, right):
    return jnp.dot(left, right, preferred_element_type=jnp.float32)


def dot3(left, right):
    (left_high, left_low), (right_high, right_low) = left, right
    return dot(left_high, right_high) + dot(left_low, right_high) + dot(left_high, right_low)


def whole(shape):
    return pl.BlockSpec(shape, lambda *_: (0,) * len(shape))


SMEM = pl.BlockSpec(memory_space=pltpu.SMEM)


def cost(flops, size):
    return pl.CostEstimate(flops=flops, bytes_accessed=size, transcendentals=0)


def eye(size):
    row = lax.broadcasted_iota(jnp.int32, (size, size), 0)
    column = lax.broadcasted_iota(jnp.int32, (size, size), 1)
    return jnp.where(row == column, 1.0, 0.0).astype(jnp.float32)


def first_gram_kernel(one, two, total, norm):
    @pl.when(pl.program_id(0) == 0)
    def _():
        total[...] = jnp.zeros_like(total)
        norm[...] = jnp.zeros_like(norm)

    width = one.shape[1]
    turned = one[...].T
    came = two[...]
    total[:width, :] += dot3(split(turned), split(came))
    total[width:, :] += jnp.sum((came * came).reshape(-1, 8, width), axis=0)
    norm[...] += jnp.broadcast_to(jnp.sum(turned * turned, axis=1, keepdims=True), norm.shape)


def first_gram(snapshots, width):
    rows = snapshots.shape[0]
    return pl.pallas_call(
        first_gram_kernel,
        grid=(rows // BLOCK,),
        in_specs=[pl.BlockSpec((BLOCK, width), lambda i: (i, 0)), pl.BlockSpec((BLOCK, width), lambda i: (i, 1))],
        out_specs=[whole((width + 8, width)), whole((width, 128))],
        out_shape=[
            jax.ShapeDtypeStruct((width + 8, width), jnp.float32),
            jax.ShapeDtypeStruct((width, 128), jnp.float32),
        ],
        compiler_params=PARAMS,
        name="first_gram",
    )(snapshots, snapshots)


def gram_kernel(turned, came, before, total):
    width = came.shape[1]
    value = came[...]
    gram = dot3(split(turned[...]), split(value))
    norm = jnp.sum((value * value).reshape(-1, 8, width), axis=0)
    if before is None:
        total[:width, :] = gram
        total[width:, :] = norm
    else:
        total[:width, :] = before[:width, :] + gram
        total[width:, :] = before[width:, :] + norm


def gram(turned, came, before):
    rows, width = came.shape
    body = gram_kernel if before is not None else lambda a, b, c: gram_kernel(a, b, None, c)
    args = (turned, came) if before is None else (turned, came, before)
    return pl.pallas_call(
        body,
        out_shape=jax.ShapeDtypeStruct((width + 8, width), jnp.float32),
        compiler_params=PARAMS,
        cost_estimate=cost(6 * rows * width * width, 4 * (2 * rows * width + 2 * width * width)),
        name="gram",
    )(*args)


def rotation_kernel(flags, mine, other, norm, stay, move, high, low, sent):
    width = stay.shape[1]
    total = mine[...] + other[...]
    norm_move = jnp.sum(total[width:, :], axis=0, keepdims=True)
    coupled = total[:width, :] / (norm[:, :1] + norm_move + EPSILON)
    turned = coupled.T
    stay_first = flags[0] == 1
    send_is_stay = flags[1] == 1
    coupling = jnp.where(stay_first, coupled, turned)
    coupling_turned = jnp.where(stay_first, turned, coupled)
    identity = eye(width)
    scale = 1.0 / (1.0 + jnp.sum(coupled * coupled))
    left, right = split(coupling_turned), split(coupling)
    base = scale * (identity + dot3(right, left))
    inverse = scale * (2.0 * identity - base)
    base_split = split(base)
    base = 2.0 * base - dot3(base_split, base_split)
    for sweep in range(1, NS_ITERS):
        base_split = split(base)
        inverse = 2.0 * inverse - dot3(split(inverse), base_split)
        if sweep < NS_ITERS - 1:
            base = 2.0 * base - dot3(base_split, base_split)
    product_turned = dot3(left, split(inverse))
    second_second = identity - 2.0 * dot3(split(product_turned), right)
    first_first = 2.0 * inverse - identity
    first_second = 2.0 * product_turned.T
    second_first = -2.0 * product_turned
    stay_stay = jnp.where(stay_first, first_first, second_second)
    move_move = jnp.where(stay_first, second_second, first_first)
    stay_move = jnp.where(stay_first, first_second, second_first)
    move_stay = jnp.where(stay_first, second_first, first_second)
    top_sent, top_sent_low = split(jnp.where(send_is_stay, stay_stay, stay_move))
    end_sent, end_sent_low = split(jnp.where(send_is_stay, move_stay, move_move))
    sent[...] = dot3(split(stay[...]), (top_sent, top_sent_low)) + dot3(split(move[...]), (end_sent, end_sent_low))
    top_kept, top_kept_low = split(jnp.where(send_is_stay, stay_move, stay_stay))
    end_kept, end_kept_low = split(jnp.where(send_is_stay, move_move, move_stay))
    high[:width, :width] = top_sent
    high[width:, :width] = end_sent
    high[:width, width:] = top_kept
    high[width:, width:] = end_kept
    low[:width, :width] = top_sent_low
    low[width:, :width] = end_sent_low
    low[:width, width:] = top_kept_low
    low[width:, width:] = end_kept_low


def view(source, block, grid_of_one):
    array, row, column = source
    if grid_of_one:
        return pl.BlockSpec(block, lambda *_: (row, column))
    return pl.BlockSpec(block, lambda i, *_: (row + i, column))


def rotation(flags, mine, other, norm, stay, move, blocks):
    width = mine.shape[1]
    size = (blocks * BLOCK, width)
    return pl.pallas_call(
        rotation_kernel,
        grid=(1,),
        in_specs=[SMEM, whole(mine.shape), whole(other.shape), whole(norm.shape), view(stay, size, True), view(move, size, True)],
        out_specs=[whole((2 * width, 2 * width)), whole((2 * width, 2 * width)), whole(size)],
        out_shape=[
            jax.ShapeDtypeStruct((2 * width, 2 * width), jnp.bfloat16),
            jax.ShapeDtypeStruct((2 * width, 2 * width), jnp.bfloat16),
            jax.ShapeDtypeStruct(size, jnp.float32),
        ],
        compiler_params=PARAMS,
        name="rotation",
    )(flags, mine, other, norm, stay[0], move[0])


def apply_kernel(first, with_sent, stay, move, high, low, *refs):
    if not first:
        before, *refs = refs
    if with_sent:
        sent, *refs = refs
    kept, turned, norm = refs
    width = stay.shape[1]
    lead = 0 if with_sent else width
    joined = jnp.concatenate((stay[...], move[...]), axis=1)
    result = dot3(split(joined), (high[:, lead:], low[:, lead:]))
    if with_sent:
        sent[...] = result[:, :width]
        result = result[:, width:]
    kept[...] = result
    result = result.T
    turned[...] = result
    squares = jnp.broadcast_to(jnp.sum(result * result, axis=1, keepdims=True), norm.shape)
    step = pl.program_id(0)

    @pl.when(step == 0)
    def _():
        norm[...] = squares if first else before[...] + squares

    @pl.when(step > 0)
    def _():
        norm[...] += squares


def apply(stay, move, high, low, before, blocks, with_sent):
    width = high.shape[0] // 2
    rows = blocks * BLOCK
    block = (BLOCK, width)
    by_row = pl.BlockSpec(block, lambda i: (i, 0))
    by_column = pl.BlockSpec((width, BLOCK), lambda i: (0, i))
    norm = whole((width, 128))
    piece = jax.ShapeDtypeStruct((rows, width), jnp.float32)
    first = before is None
    return pl.pallas_call(
        functools.partial(apply_kernel, first, with_sent),
        grid=(blocks,),
        in_specs=[view(stay, block, False), view(move, block, False), whole(high.shape), whole(low.shape)]
        + [norm] * (not first),
        out_specs=[by_row] * with_sent + [by_row, by_column, norm],
        out_shape=[piece] * with_sent
        + [piece, jax.ShapeDtypeStruct((width, rows), jnp.float32), jax.ShapeDtypeStruct((width, 128), jnp.float32)],
        compiler_params=PARAMS,
        cost_estimate=cost(24 * rows * width * width, 20 * rows * width),
        name="apply",
    )(stay[0], move[0], high, low, *([] if first else [before]))


def last_apply_kernel(first, with_sent, place, stay, move, high, low, *refs):
    if not first:
        before, *refs = refs
    width = stay.shape[1]
    lead = 0 if with_sent else width
    joined = jnp.concatenate((stay[...], move[...]), axis=1)
    result = dot3(split(joined), (high[:, lead:], low[:, lead:]))
    if with_sent:
        refs[0][...] = result[:, :width]
        result = result[:, width:]
    refs[-1][...] = result


def last_apply(place, stay, move, high, low, before, start, blocks, shape, with_sent):
    width = high.shape[0] // 2
    block = (BLOCK, width)
    first = before is None
    out = pl.BlockSpec(block, lambda i, place: (start + i, place[0]))
    by_row = pl.BlockSpec(block, lambda i, place: (i, 0))
    rows = blocks * BLOCK
    return pl.pallas_call(
        functools.partial(last_apply_kernel, first, with_sent),
        grid_spec=pltpu.PrefetchScalarGridSpec(
            num_scalar_prefetch=1,
            grid=(blocks,),
            in_specs=[view(stay, block, False), view(move, block, False), whole(high.shape), whole(low.shape)]
            + [pl.BlockSpec(memory_space=pl.ANY)] * (not first),
            out_specs=[by_row] * with_sent + [out],
        ),
        out_shape=[jax.ShapeDtypeStruct((rows, width), jnp.float32)] * with_sent
        + [jax.ShapeDtypeStruct(shape, jnp.float32)],
        input_output_aliases={} if first else {5: 1 if with_sent else 0},
        compiler_params=PARAMS,
        cost_estimate=cost(24 * rows * width * width, 20 * rows * width),
        name="last_apply",
    )(place, stay[0], move[0], high, low, *([] if first else [before]))


def place_kernel(place, came, before, out):
    out[...] = came[...]


def put(place, came, before, start):
    rows, width = came.shape
    block = (BLOCK, width)
    return pl.pallas_call(
        place_kernel,
        grid_spec=pltpu.PrefetchScalarGridSpec(
            num_scalar_prefetch=1,
            grid=(rows // BLOCK,),
            in_specs=[pl.BlockSpec(block, lambda i, place: (i, 0)), pl.BlockSpec(memory_space=pl.ANY)],
            out_specs=pl.BlockSpec(block, lambda i, place: (start + i, place[0])),
        ),
        out_shape=jax.ShapeDtypeStruct(before.shape, jnp.float32),
        input_output_aliases={2: 0},
        compiler_params=PARAMS,
        cost_estimate=cost(0, 8 * rows * width),
        name="put",
    )(place, came, before)


def per_device(snapshots, plan):
    rows = snapshots.shape[0]
    width = snapshots.shape[1] // 2
    rounds = plan.shape[0]
    blocks = rows // BLOCK
    sizes = [share * blocks // sum(PIECES) for share in PIECES]
    starts = [sum(sizes[:i]) for i in range(len(sizes))]
    device = lax.axis_index("pair")
    count = lax.axis_size("pair")
    stay = [(snapshots, start, 0) for start in starts]
    move = [(snapshots, start, 1) for start in starts]
    stay_first = jnp.bool_(True)
    for round_index in range(rounds):
        last = round_index == rounds - 1
        odd = round_index % 2
        position = (device + odd) % count
        upper = (position + 1) % count
        layout = plan[round_index]
        upper_zero = lax.dynamic_index_in_dim(layout, 2 * upper, 0, False)
        upper_one = lax.dynamic_index_in_dim(layout, 2 * upper + 1, 0, False)
        second_goes_up = (upper_zero == 2 * position + 1) | (upper_one == 2 * position + 1)
        send_is_second = second_goes_up if odd else ~second_goes_up
        send_is_stay = send_is_second != stay_first
        flags = jnp.stack((stay_first, send_is_stay)).astype(jnp.int32)
        target = device if odd else (device + 1) % count
        below = (target + count - 1) % count
        source_zero = lax.dynamic_index_in_dim(layout, 2 * target, 0, False)
        zero_from_below = source_zero // 2 == below
        stay_first = ~zero_from_below if odd else zero_from_below

        if round_index == 0:
            total, norm = first_gram(snapshots, width)
            norm = norm + shift(norm, "row", 1)
        else:
            total = None
            for one, two in zip(turned, move):
                total = gram(one, two[0], total)
        other = shift(total, "row", 1)
        high, low, outgoing = rotation(flags, total, other, norm, stay[0], move[0], sizes[0])

        direction = 2 if odd else -2
        arriving = [shift(outgoing, "pair", direction)]
        if last and rounds % 2 == 0:
            stay_column = jnp.where(stay_first, 0, 1).astype(jnp.int32)[None]
            field = None
            for piece in range(1, len(sizes)):
                outgoing, field = last_apply(
                    stay_column, stay[piece], move[piece], high, low, field, starts[piece], sizes[piece], snapshots.shape, True
                )
                arriving.append(shift(outgoing, "pair", direction))
            (field,) = last_apply(
                stay_column, stay[0], move[0], high, low, field, starts[0], sizes[0], snapshots.shape, False
            )
            for piece, start in zip(arriving, starts):
                field = put(1 - stay_column, piece, field, start)
            return field
        norm = None
        held = [None] * len(sizes)
        for piece in range(1, len(sizes)):
            outgoing, *held[piece], norm = apply(stay[piece], move[piece], high, low, norm, sizes[piece], True)
            arriving.append(shift(outgoing, "pair", direction))
        *held[0], norm = apply(stay[0], move[0], high, low, norm, sizes[0], False)
        stay = [(kept, 0, 0) for kept, _ in held]
        turned = [value for _, value in held]
        move = [(value, 0, 0) for value in arriving]
        norm = norm + shift(norm, "row", 1)
    stay = shift(jnp.concatenate([value for value, _, _ in stay], axis=0), "pair", 1)
    move = shift(jnp.concatenate([value for value, _, _ in move], axis=0), "pair", 1)
    stay_first = shift(stay_first.astype(jnp.int32), "pair", 1) == 1
    return jnp.concatenate(
        (jnp.where(stay_first, stay, move), jnp.where(stay_first, move, stay)), axis=1
    )


def solution(mesh):
    in_specs = (P(("basin", "row"), "pair"), P())
    out_specs = P(("basin", "row"), "pair")
    return jax.shard_map(
        per_device, mesh=mesh, in_specs=in_specs, out_specs=out_specs, check_vma=False
    )
```

profile of v0, /device:TPU:0, one launch (start us, length us, event | category | flops | bytes accessed | tf_op | source)
XLA Modules:
  0.0 258.4 jit_solution(3335369979482404737)
XLA Ops:
  0.0 2.2 copy-done
  2.2 3.0 %first_gram.1 = (f32[264,256]{1,0:T(8,128)S(1)}, f32[256,128]{1,0:T(8,128)S(1)}) custom-call(f32[2048,512]{1,0:T(8,128)S(1)} %copy-done, f32[2048,512]{1,0:T(8,128)S(1)} %copy-done), custom_call_target="tpu_custom_call" | custom-call | tf_op jit(solution)/shard_map/first_gram/pallas_call | solution.py:69
  5.8 0.7 constant_dynamic-slice_fusion.5
  8.0 2.2 copy-done.1
  10.1 4.3 %rotation.4 = (bf16[512,512]{1,0:T(8,128)(2,1)S(1)}, bf16[512,512]{1,0:T(8,128)(2,1)S(1)}, f32[256,256]{1,0:T(8,128)S(1)}) custom-call(s32[2]{0:T(128)S(1)} %add_convert_fusion.flags, f32[264,256]{1,0:T(8,128)S(1)} %get-tuple-element.70.mine, f32[264,256]{1,0:T(8,128)S(1)} %collective-permute-done.other, f32[256,128]{1,0:T(8,128)S(1)} %add.125.norm, ...), custom_call_target="tpu_custom_call" | custom-call | tf_op jit(solution)/shard_map/rotation/pallas_call | solution.py:165
  14.4 2.4 apply.12
  16.9 5.1 %collective-permute-start.4 = (f32[768,256]{1,0:T(8,128)S(1)}, f32[768,256]{1,0:T(8,128)S(1)}, u32[]{:S(2)}, u32[]{:S(2)}) collective-permute-start(f32[768,256]{1,0:T(8,128)S(1)} %get-tuple-element.82), channel_id=1, source_target_pairs={{0,12},{2,14},{4,0},{6,2},{8,4},{10,6},{12,8},{14,10},{1,13},{3,15... | collective-permute-start | bytes 2359304 | tf_op jit(solution)/shard_map/ppermute | solution.py:19
  21.9 2.4 apply.13
  25.3 0.7 apply.14
  26.7 35.6 %collective-permute-done.5.b.move = f32[256,256]{1,0:T(8,128)S(1)} collective-permute-done((f32[256,256]{1,0:T(8,128)S(1)}, f32[256,256]{1,0:T(8,128)S(1)}, u32[]{:S(2)}, u32[]{:S(2)}) %collective-permute-start.5) | collective-permute-done | bytes 262176 | tf_op jit(solution)/shard_map/ppermute | solution.py:19
  63.6 3.5 %collective-permute-done.2.came.move = f32[256,256]{1,0:T(8,128)S(1)} collective-permute-done((f32[256,256]{1,0:T(8,128)S(1)}, f32[256,256]{1,0:T(8,128)S(1)}, u32[]{:S(2)}, u32[]{:S(2)}) %collective-permute-start.2) | collective-permute-done | bytes 262176 | tf_op jit(solution)/shard_map/ppermute | solution.py:19
  72.2 4.3 %rotation.5 = (bf16[512,512]{1,0:T(8,128)(2,1)S(1)}, bf16[512,512]{1,0:T(8,128)(2,1)S(1)}, f32[256,256]{1,0:T(8,128)S(1)}) custom-call(s32[2]{0:T(128)S(1)} %add_convert_fusion.1.flags, f32[264,256]{1,0:T(8,128)S(1)} %gram.15.mine, f32[264,256]{1,0:T(8,128)S(1)} %collective-permute-done.6.other, f32[256,128]{1,0:T(8,128)S(1)} %add.136.norm, ...), custom_call_target="tpu_custom_call" | custom-call | tf_op jit(solution)/shard_map/rotation/pallas_call | solution.py:165
  76.5 1.1 copy-done.11
  77.6 2.3 apply.16
  79.9 0.9 copy-done.16
  81.3 1.1 copy-done.9
  82.4 2.3 apply.17
  84.7 1.6 collective-permute-start.9
  86.4 3.4 %collective-permute-start.11 = (f32[256,256]{1,0:T(8,128)S(1)}, f32[256,256]{1,0:T(8,128)S(1)}, u32[]{:S(2)}, u32[]{:S(2)}) collective-permute-start(f32[256,256]{1,0:T(8,128)S(1)} %get-tuple-element.103), channel_id=1, source_target_pairs={{0,4},{2,6},{4,8},{6,10},{8,12},{10,14},{12,0},{14,2},{1,5},{3,7},... | collective-permute-start | bytes 786440 | tf_op jit(solution)/shard_map/ppermute | solution.py:19
  89.7 0.7 apply.18
  91.3 34.6 %collective-permute-done.11.b.move = f32[256,256]{1,0:T(8,128)S(1)} collective-permute-done((f32[256,256]{1,0:T(8,128)S(1)}, f32[256,256]{1,0:T(8,128)S(1)}, u32[]{:S(2)}, u32[]{:S(2)}) %collective-permute-start.11) | collective-permute-done | bytes 262176 | tf_op jit(solution)/shard_map/ppermute | solution.py:19
  127.2 3.7 %collective-permute-done.8.came.move = f32[256,256]{1,0:T(8,128)S(1)} collective-permute-done((f32[256,256]{1,0:T(8,128)S(1)}, f32[256,256]{1,0:T(8,128)S(1)}, u32[]{:S(2)}, u32[]{:S(2)}) %collective-permute-start.8) | collective-permute-done | bytes 262176 | tf_op jit(solution)/shard_map/ppermute | solution.py:19
  134.1 0.7 constant_dynamic-slice_fusion
  136.3 4.3 %rotation.6 = (bf16[512,512]{1,0:T(8,128)(2,1)S(1)}, bf16[512,512]{1,0:T(8,128)(2,1)S(1)}, f32[256,256]{1,0:T(8,128)S(1)}) custom-call(s32[2]{0:T(128)S(1)} %add_convert_fusion.2.flags, f32[264,256]{1,0:T(8,128)S(1)} %gram.19.mine, f32[264,256]{1,0:T(8,128)S(1)} %collective-permute-done.12.other, f32[256,128]{1,0:T(8,128)S(1)} %add.137.norm, ...), custom_call_target="tpu_custom_call" | custom-call | tf_op jit(solution)/shard_map/rotation/pallas_call | solution.py:165
  140.6 1.1 copy-done.17
  141.7 2.3 apply.20
  144.0 0.9 copy-done.14
  144.9 1.7 collective-permute-start.16
  146.6 1.1 copy-done.13
  147.7 2.3 apply.21
  150.2 0.7 apply.22
  150.9 3.2 %collective-permute-start.14 = (f32[256,256]{1,0:T(8,128)S(1)}, f32[256,256]{1,0:T(8,128)S(1)}, u32[]{:S(2)}, u32[]{:S(2)}) collective-permute-start(f32[256,256]{1,0:T(8,128)S(1)} %get-tuple-element.113), channel_id=1, source_target_pairs={{0,12},{2,14},{4,0},{6,2},{8,4},{10,6},{12,8},{14,10},{1,13},{3,15... | collective-permute-start | bytes 786440 | tf_op jit(solution)/shard_map/ppermute | solution.py:19
  154.7 33.1 %collective-permute-done.17.b.move = f32[256,256]{1,0:T(8,128)S(1)} collective-permute-done((f32[256,256]{1,0:T(8,128)S(1)}, f32[256,256]{1,0:T(8,128)S(1)}, u32[]{:S(2)}, u32[]{:S(2)}) %collective-permute-start.17) | collective-permute-done | bytes 262176 | tf_op jit(solution)/shard_map/ppermute | solution.py:19
  189.1 3.4 %collective-permute-done.14.came.move = f32[256,256]{1,0:T(8,128)S(1)} collective-permute-done((f32[256,256]{1,0:T(8,128)S(1)}, f32[256,256]{1,0:T(8,128)S(1)}, u32[]{:S(2)}, u32[]{:S(2)}) %collective-permute-start.14) | collective-permute-done | bytes 262176 | tf_op jit(solution)/shard_map/ppermute | solution.py:19
  200.3 4.3 %rotation.7 = (bf16[512,512]{1,0:T(8,128)(2,1)S(1)}, bf16[512,512]{1,0:T(8,128)(2,1)S(1)}, f32[256,256]{1,0:T(8,128)S(1)}) custom-call(s32[2]{0:T(128)S(1)} %add_convert_fusion.3.flags, f32[264,256]{1,0:T(8,128)S(1)} %gram.23.mine, f32[264,256]{1,0:T(8,128)S(1)} %collective-permute-done.18.other, f32[256,128]{1,0:T(8,128)S(1)} %add.138.norm, ...), custom_call_target="tpu_custom_call" | custom-call | tf_op jit(solution)/shard_map/rotation/pallas_call | solution.py:165
  204.6 1.1 copy-done.15
  205.7 2.6 %last_apply.4 = (f32[768,256]{1,0:T(8,128)S(1)}, f32[2048,512]{1,0:T(8,128)}) custom-call(s32[1]{0:T(128)} %bitcast.1.place, f32[768,256]{1,0:T(8,128)S(1)} %copy-done.15, f32[768,256]{1,0:T(8,128)S(1)} %collective-permute-done.16.came.move, bf16[512,512]{1,0:T(8,128)(2,1)S(1)} %get-tuple-element.124.high, bf16[512,512]{1,0:T(8,128)(2,1)S(1)} %get-tuple-element.125.low), custom_call_target="tpu_custom_call" | custom-call | flops 1207959552 | bytes 3932160 | tf_op jit(solution)/shard_map/last_apply/pallas_call | solution.py:251
  208.3 2.6 %last_apply.5 = (f32[768,256]{1,0:T(8,128)S(1)}, f32[2048,512]{1,0:T(8,128)}) custom-call(s32[1]{0:T(128)} %bitcast.1.place, f32[768,256]{1,0:T(8,128)S(1)} %copy-done.7, f32[768,256]{1,0:T(8,128)S(1)} %collective-permute-done.15.came.move, bf16[512,512]{1,0:T(8,128)(2,1)S(1)} %get-tuple-element.124.high, ...), custom_call_target="tpu_custom_call", output_to_operand_aliasing={{1}: (5, {})} | custom-call | flops 1207959552 | bytes 3932160 | tf_op jit(solution)/shard_map/last_apply/pallas_call | solution.py:251
  210.9 1.1 collective-permute-start.21
  212.0 3.5 %collective-permute-start.23 = (f32[256,256]{1,0:T(8,128)S(1)}, f32[256,256]{1,0:T(8,128)S(1)}, u32[]{:S(2)}, u32[]{:S(2)}) collective-permute-start(f32[256,256]{1,0:T(8,128)S(1)} %get-tuple-element.133), channel_id=1, source_target_pairs={{0,4},{2,6},{4,8},{6,10},{8,12},{10,14},{12,0},{14,2},{1,5},{3,7},... | collective-permute-start | bytes 786440 | tf_op jit(solution)/shard_map/ppermute | solution.py:19
  215.5 1.3 last_apply.6
  217.1 1.1 last_apply.7.before
  218.2 34.7 %collective-permute-done.23.came = f32[256,256]{1,0:T(8,128)S(1)} collective-permute-done((f32[256,256]{1,0:T(8,128)S(1)}, f32[256,256]{1,0:T(8,128)S(1)}, u32[]{:S(2)}, u32[]{:S(2)}) %collective-permute-start.23) | collective-permute-done | bytes 262176 | tf_op jit(solution)/shard_map/ppermute | solution.py:19
  252.9 0.7 put.4.before
  253.7 1.4 put.5.before
  255.1 1.4 put.6.before
  256.5 1.1 collective-permute-done.20.came
  257.7 0.7 put.7
  (86 shorter events, 11.1 us)
Async XLA Ops:
  0.0 2.2 copy-start
  2.2 3.6 %copy-start.18 = (s32[4,16]{1,0:T(4,128)S(1)}, s32[4,16]{1,0:T(4,128)}, u32[]{:S(2)}) copy-start(s32[4,16]{1,0:T(4,128)} %param.3) | copy-start | bytes 772
  5.2 2.7 %collective-permute-start.1 = (f32[256,128]{1,0:T(8,128)S(1)}, f32[256,128]{1,0:T(8,128)S(1)}, u32[]{:S(2)}, u32[]{:S(2)}) collective-permute-start(f32[256,128]{1,0:T(8,128)S(1)} %get-tuple-element.71), channel_id=1, source_target_pairs={{0,1},{1,0},{2,3},{3,2},{4,5},{5,4},{6,7},{7,6},{8,9},{9,8},{10,11... | collective-permute-start | bytes 393224 | tf_op jit(solution)/shard_map/ppermute | solution.py:19
  5.7 2.2 collective-permute-start
  7.9 2.2 copy-start.1
  16.8 7.5 %copy-start.10 = (f32[768,256]{1,0:T(8,128)}, f32[768,256]{1,0:T(8,128)S(1)}, u32[]{:S(2)}) copy-start(f32[768,256]{1,0:T(8,128)S(1)} %get-tuple-element.91.stay) | copy-start | bytes 2359300
  16.9 45.7 %collective-permute-start.4 = (f32[768,256]{1,0:T(8,128)S(1)}, f32[768,256]{1,0:T(8,128)S(1)}, u32[]{:S(2)}, u32[]{:S(2)}) collective-permute-start(f32[768,256]{1,0:T(8,128)S(1)} %get-tuple-element.82), channel_id=1, source_target_pairs={{0,12},{2,14},{4,0},{6,2},{8,4},{10,6},{12,8},{14,10},{1,13},{3,15... | collective-permute-start | bytes 2359304 | tf_op jit(solution)/shard_map/ppermute | solution.py:19
  24.4 1.7 copy-start.8
  24.4 38.7 %collective-permute-start.3 = (f32[768,256]{1,0:T(8,128)S(1)}, f32[768,256]{1,0:T(8,128)S(1)}, u32[]{:S(2)}, u32[]{:S(2)}) collective-permute-start(f32[768,256]{1,0:T(8,128)S(1)} %get-tuple-element.80), channel_id=1, source_target_pairs={{0,12},{2,14},{4,0},{6,2},{8,4},{10,6},{12,8},{14,10},{1,13},{3,15... | collective-permute-start | bytes 2359304 | tf_op jit(solution)/shard_map/ppermute | solution.py:19
  24.9 37.4 %collective-permute-start.5 = (f32[256,256]{1,0:T(8,128)S(1)}, f32[256,256]{1,0:T(8,128)S(1)}, u32[]{:S(2)}, u32[]{:S(2)}) collective-permute-start(f32[256,256]{1,0:T(8,128)S(1)} %get-tuple-element.85), channel_id=1, source_target_pairs={{0,12},{2,14},{4,0},{6,2},{8,4},{10,6},{12,8},{14,10},{1,13},{3,15... | collective-permute-start | bytes 786440 | tf_op jit(solution)/shard_map/ppermute | solution.py:19
  26.1 41.0 %collective-permute-start.2 = (f32[256,256]{1,0:T(8,128)S(1)}, f32[256,256]{1,0:T(8,128)S(1)}, u32[]{:S(2)}, u32[]{:S(2)}) collective-permute-start(f32[256,256]{1,0:T(8,128)S(1)} %get-tuple-element.77), channel_id=1, source_target_pairs={{0,12},{2,14},{4,0},{6,2},{8,4},{10,6},{12,8},{14,10},{1,13},{3,15... | collective-permute-start | bytes 786440 | tf_op jit(solution)/shard_map/ppermute | solution.py:19
  63.1 4.3 %copy-start.4 = (f32[768,256]{1,0:T(8,128)}, f32[768,256]{1,0:T(8,128)S(1)}, u32[]{:S(2)}) copy-start(f32[768,256]{1,0:T(8,128)S(1)} %collective-permute-done.3.came.move) | copy-start | bytes 2359300
  67.4 4.8 %collective-permute-start.6 = (f32[264,256]{1,0:T(8,128)S(1)}, f32[264,256]{1,0:T(8,128)S(1)}, u32[]{:S(2)}, u32[]{:S(2)}) collective-permute-start(f32[264,256]{1,0:T(8,128)S(1)} %gram.15.mine), channel_id=1, source_target_pairs={{0,1},{1,0},{2,3},{3,2},{4,5},{5,4},{6,7},{7,6},{8,9},{9,8},{10,11... | collective-permute-start | bytes 811016 | tf_op jit(solution)/shard_map/ppermute | solution.py:19
  67.4 4.7 %collective-permute-start.7 = (f32[256,128]{1,0:T(8,128)S(1)}, f32[256,128]{1,0:T(8,128)S(1)}, u32[]{:S(2)}, u32[]{:S(2)}) collective-permute-start(f32[256,128]{1,0:T(8,128)S(1)} %get-tuple-element.86), channel_id=1, source_target_pairs={{0,1},{1,0},{2,3},{3,2},{4,5},{5,4},{6,7},{7,6},{8,9},{9,8},{10,11... | collective-permute-start | bytes 393224 | tf_op jit(solution)/shard_map/ppermute | solution.py:19
  72.1 9.2 %copy-start.5 = (f32[768,256]{1,0:T(8,128)S(1)}, f32[768,256]{1,0:T(8,128)}, u32[]{:S(2)}) copy-start(f32[768,256]{1,0:T(8,128)} %copy-done.4) | copy-start | bytes 2359300
  76.5 1.1 copy-start.11
  79.9 0.9 copy-start.16
  80.8 45.4 %collective-permute-start.10 = (f32[768,256]{1,0:T(8,128)S(1)}, f32[768,256]{1,0:T(8,128)S(1)}, u32[]{:S(2)}, u32[]{:S(2)}) collective-permute-start(f32[768,256]{1,0:T(8,128)S(1)} %get-tuple-element.100), channel_id=1, source_target_pairs={{0,4},{2,6},{4,8},{6,10},{8,12},{10,14},{12,0},{14,2},{1,5},{3,7},... | collective-permute-start | bytes 2359304 | tf_op jit(solution)/shard_map/ppermute | solution.py:19
  81.3 1.1 copy-start.9
  84.7 41.2 %copy-start.12 = (f32[768,256]{1,0:T(8,128)}, f32[768,256]{1,0:T(8,128)S(1)}, u32[]{:S(2)}) copy-start(f32[768,256]{1,0:T(8,128)S(1)} %get-tuple-element.108.stay) | copy-start | bytes 2359300
  84.7 42.0 %collective-permute-start.9 = (f32[768,256]{1,0:T(8,128)S(1)}, f32[768,256]{1,0:T(8,128)S(1)}, u32[]{:S(2)}, u32[]{:S(2)}) collective-permute-start(f32[768,256]{1,0:T(8,128)S(1)} %get-tuple-element.98), channel_id=1, source_target_pairs={{0,4},{2,6},{4,8},{6,10},{8,12},{10,14},{12,0},{14,2},{1,5},{3,7},... | collective-permute-start | bytes 2359304 | tf_op jit(solution)/shard_map/ppermute | solution.py:19
  86.4 39.5 %collective-permute-start.11 = (f32[256,256]{1,0:T(8,128)S(1)}, f32[256,256]{1,0:T(8,128)S(1)}, u32[]{:S(2)}, u32[]{:S(2)}) collective-permute-start(f32[256,256]{1,0:T(8,128)S(1)} %get-tuple-element.103), channel_id=1, source_target_pairs={{0,4},{2,6},{4,8},{6,10},{8,12},{10,14},{12,0},{14,2},{1,5},{3,7},... | collective-permute-start | bytes 786440 | tf_op jit(solution)/shard_map/ppermute | solution.py:19
  90.5 40.5 %collective-permute-start.8 = (f32[256,256]{1,0:T(8,128)S(1)}, f32[256,256]{1,0:T(8,128)S(1)}, u32[]{:S(2)}, u32[]{:S(2)}) collective-permute-start(f32[256,256]{1,0:T(8,128)S(1)} %get-tuple-element.95), channel_id=1, source_target_pairs={{0,4},{2,6},{4,8},{6,10},{8,12},{10,14},{12,0},{14,2},{1,5},{3,7},... | collective-permute-start | bytes 786440 | tf_op jit(solution)/shard_map/ppermute | solution.py:19
  126.7 4.5 %copy-start.2 = (f32[768,256]{1,0:T(8,128)}, f32[768,256]{1,0:T(8,128)S(1)}, u32[]{:S(2)}) copy-start(f32[768,256]{1,0:T(8,128)S(1)} %collective-permute-done.9.came.move) | copy-start | bytes 2359300
  131.2 5.0 %collective-permute-start.12 = (f32[264,256]{1,0:T(8,128)S(1)}, f32[264,256]{1,0:T(8,128)S(1)}, u32[]{:S(2)}, u32[]{:S(2)}) collective-permute-start(f32[264,256]{1,0:T(8,128)S(1)} %gram.19.mine), channel_id=1, source_target_pairs={{0,1},{1,0},{2,3},{3,2},{4,5},{5,4},{6,7},{7,6},{8,9},{9,8},{10,11... | collective-permute-start | bytes 811016 | tf_op jit(solution)/shard_map/ppermute | solution.py:19
  131.3 4.9 %collective-permute-start.13 = (f32[256,128]{1,0:T(8,128)S(1)}, f32[256,128]{1,0:T(8,128)S(1)}, u32[]{:S(2)}, u32[]{:S(2)}) collective-permute-start(f32[256,128]{1,0:T(8,128)S(1)} %get-tuple-element.104), channel_id=1, source_target_pairs={{0,1},{1,0},{2,3},{3,2},{4,5},{5,4},{6,7},{7,6},{8,9},{9,8},{10,11... | collective-permute-start | bytes 393224 | tf_op jit(solution)/shard_map/ppermute | solution.py:19
  136.2 10.4 %copy-start.3 = (f32[768,256]{1,0:T(8,128)S(1)}, f32[768,256]{1,0:T(8,128)}, u32[]{:S(2)}) copy-start(f32[768,256]{1,0:T(8,128)} %copy-done.2) | copy-start | bytes 2359300
  140.5 1.1 copy-start.17
  144.0 0.9 copy-start.14
  144.9 43.2 %collective-permute-start.16 = (f32[768,256]{1,0:T(8,128)S(1)}, f32[768,256]{1,0:T(8,128)S(1)}, u32[]{:S(2)}, u32[]{:S(2)}) collective-permute-start(f32[768,256]{1,0:T(8,128)S(1)} %get-tuple-element.118), channel_id=1, source_target_pairs={{0,12},{2,14},{4,0},{6,2},{8,4},{10,6},{12,8},{14,10},{1,13},{3,15... | collective-permute-start | bytes 2359304 | tf_op jit(solution)/shard_map/ppermute | solution.py:19
  146.6 1.1 copy-start.13
  150.1 39.0 %copy-start.6 = (f32[768,256]{1,0:T(8,128)}, f32[768,256]{1,0:T(8,128)S(1)}, u32[]{:S(2)}) copy-start(f32[768,256]{1,0:T(8,128)S(1)} %get-tuple-element.126.stay) | copy-start | bytes 2359300
  150.1 38.5 %collective-permute-start.15 = (f32[768,256]{1,0:T(8,128)S(1)}, f32[768,256]{1,0:T(8,128)S(1)}, u32[]{:S(2)}, u32[]{:S(2)}) collective-permute-start(f32[768,256]{1,0:T(8,128)S(1)} %get-tuple-element.116), channel_id=1, source_target_pairs={{0,12},{2,14},{4,0},{6,2},{8,4},{10,6},{12,8},{14,10},{1,13},{3,15... | collective-permute-start | bytes 2359304 | tf_op jit(solution)/shard_map/ppermute | solution.py:19
  150.1 37.6 %collective-permute-start.17 = (f32[256,256]{1,0:T(8,128)S(1)}, f32[256,256]{1,0:T(8,128)S(1)}, u32[]{:S(2)}, u32[]{:S(2)}) collective-permute-start(f32[256,256]{1,0:T(8,128)S(1)} %get-tuple-element.121), channel_id=1, source_target_pairs={{0,12},{2,14},{4,0},{6,2},{8,4},{10,6},{12,8},{14,10},{1,13},{3,15... | collective-permute-start | bytes 786440 | tf_op jit(solution)/shard_map/ppermute | solution.py:19
  150.9 41.6 %collective-permute-start.14 = (f32[256,256]{1,0:T(8,128)S(1)}, f32[256,256]{1,0:T(8,128)S(1)}, u32[]{:S(2)}, u32[]{:S(2)}) collective-permute-start(f32[256,256]{1,0:T(8,128)S(1)} %get-tuple-element.113), channel_id=1, source_target_pairs={{0,12},{2,14},{4,0},{6,2},{8,4},{10,6},{12,8},{14,10},{1,13},{3,15... | collective-permute-start | bytes 786440 | tf_op jit(solution)/shard_map/ppermute | solution.py:19
  192.8 7.5 %collective-permute-start.18 = (f32[264,256]{1,0:T(8,128)S(1)}, f32[264,256]{1,0:T(8,128)S(1)}, u32[]{:S(2)}, u32[]{:S(2)}) collective-permute-start(f32[264,256]{1,0:T(8,128)S(1)} %gram.23.mine), channel_id=1, source_target_pairs={{0,1},{1,0},{2,3},{3,2},{4,5},{5,4},{6,7},{7,6},{8,9},{9,8},{10,11... | collective-permute-start | bytes 811016 | tf_op jit(solution)/shard_map/ppermute | solution.py:19
  192.9 7.4 %collective-permute-start.19 = (f32[256,128]{1,0:T(8,128)S(1)}, f32[256,128]{1,0:T(8,128)S(1)}, u32[]{:S(2)}, u32[]{:S(2)}) collective-permute-start(f32[256,128]{1,0:T(8,128)S(1)} %get-tuple-element.122), channel_id=1, source_target_pairs={{0,1},{1,0},{2,3},{3,2},{4,5},{5,4},{6,7},{7,6},{8,9},{9,8},{10,11... | collective-permute-start | bytes 393224 | tf_op jit(solution)/shard_map/ppermute | solution.py:19
  200.2 8.1 %copy-start.7 = (f32[768,256]{1,0:T(8,128)S(1)}, f32[768,256]{1,0:T(8,128)}, u32[]{:S(2)}) copy-start(f32[768,256]{1,0:T(8,128)} %copy-done.6) | copy-start | bytes 2359300
  204.5 1.1 copy-start.15
  208.3 45.4 %collective-permute-start.22 = (f32[768,256]{1,0:T(8,128)S(1)}, f32[768,256]{1,0:T(8,128)S(1)}, u32[]{:S(2)}, u32[]{:S(2)}) collective-permute-start(f32[768,256]{1,0:T(8,128)S(1)} %get-tuple-element.132), channel_id=1, source_target_pairs={{0,4},{2,6},{4,8},{6,10},{8,12},{10,14},{12,0},{14,2},{1,5},{3,7},... | collective-permute-start | bytes 2359304 | tf_op jit(solution)/shard_map/ppermute | solution.py:19
  210.9 44.2 %collective-permute-start.21 = (f32[768,256]{1,0:T(8,128)S(1)}, f32[768,256]{1,0:T(8,128)S(1)}, u32[]{:S(2)}, u32[]{:S(2)}) collective-permute-start(f32[768,256]{1,0:T(8,128)S(1)} %get-tuple-element.131), channel_id=1, source_target_pairs={{0,4},{2,6},{4,8},{6,10},{8,12},{10,14},{12,0},{14,2},{1,5},{3,7},... | collective-permute-start | bytes 2359304 | tf_op jit(solution)/shard_map/ppermute | solution.py:19
  212.0 40.9 %collective-permute-start.23 = (f32[256,256]{1,0:T(8,128)S(1)}, f32[256,256]{1,0:T(8,128)S(1)}, u32[]{:S(2)}, u32[]{:S(2)}) collective-permute-start(f32[256,256]{1,0:T(8,128)S(1)} %get-tuple-element.133), channel_id=1, source_target_pairs={{0,4},{2,6},{4,8},{6,10},{8,12},{10,14},{12,0},{14,2},{1,5},{3,7},... | collective-permute-start | bytes 786440 | tf_op jit(solution)/shard_map/ppermute | solution.py:19
  216.8 40.8 %collective-permute-start.20 = (f32[256,256]{1,0:T(8,128)S(1)}, f32[256,256]{1,0:T(8,128)S(1)}, u32[]{:S(2)}, u32[]{:S(2)}) collective-permute-start(f32[256,256]{1,0:T(8,128)S(1)} %get-tuple-element.130), channel_id=1, source_target_pairs={{0,4},{2,6},{4,8},{6,10},{8,12},{10,14},{12,0},{14,2},{1,5},{3,7},... | collective-permute-start | bytes 786440 | tf_op jit(solution)/shard_map/ppermute | solution.py:19
where the time goes:
time: 259 us; the launch traced here: 258 us
  waiting for transfers between devices  150 us (58%)
  Pallas kernels  54.3 us (21%)
  starting transfers between devices  24.1 us (9%)
  between operations  16.5 us (6%)
  local copies, waits for them, and re-layouts  13.2 us (5%)
    ppermute x24, waiting for transfers between devices, shift(): lax.ppermute(value, axis, [(i, (i + by) % size) for i in range(size)])  150 us
    ppermute x24, starting transfers between devices, shift(): lax.ppermute(value, axis, [(i, (i + by) % size) for i in range(size)])  24.1 us
    pallas_call x12, Pallas kernels, apply(): pl.pallas_call(functools.partial(apply_kernel, first, with_sent), grid=(b...  17.8 us
    pallas_call x4, Pallas kernels, rotation(): pl.pallas_call(rotation_kernel, grid=(1,), in_specs=[SMEM, whole(mine.sha...  17 us
    unnamed x38, local copies, waits for them, and re-layouts  11.8 us
    pallas_call x4, Pallas kernels, last_apply(): pl.pallas_call(functools.partial(last_apply_kernel, first, with_sent), gr...  7.57 us
  transfers between devices with their start and end apart: 24, of which 8 were waited for; matrix products, arithmetic and copies ran while one was open for 1% of the time, Pallas kernels for 9%

commit v1 on v0

--- a/solution.py
+++ b/solution.py
@@ -10,8 +10,8 @@
 NS_ITERS = 6
 EPSILON = 1e-06
 BLOCK = 256
-PIECES = (1, 3, 3, 1)
-PARAMS = pltpu.CompilerParams(vmem_limit_bytes=32 * 1024 * 1024)
+PIECES = (2, 2, 2, 2)
+PARAMS = pltpu.CompilerParams(vmem_limit_bytes=12 * 1024 * 1024)
 
 
 def shift(value, axis, by):
@@ -40,8 +40,7 @@
 SMEM = pl.BlockSpec(memory_space=pltpu.SMEM)
 
 
-def cost(flops, size):
-    return pl.CostEstimate(flops=flops, bytes_accessed=size, transcendentals=0)
+COST = pl.CostEstimate(flops=1024, bytes_accessed=1024, transcendentals=0)
 
 
 def eye(size):
@@ -50,34 +49,80 @@
     return jnp.where(row == column, 1.0, 0.0).astype(jnp.float32)
 
 
-def first_gram_kernel(one, two, total, norm):
-    @pl.when(pl.program_id(0) == 0)
-    def _():
-        total[...] = jnp.zeros_like(total)
-        norm[...] = jnp.zeros_like(norm)
-
-    width = one.shape[1]
-    turned = one[...].T
-    came = two[...]
-    total[:width, :] += dot3(split(turned), split(came))
-    total[width:, :] += jnp.sum((came * came).reshape(-1, 8, width), axis=0)
-    norm[...] += jnp.broadcast_to(jnp.sum(turned * turned, axis=1, keepdims=True), norm.shape)
+def flags_kernel(count, plan, device, flags):
+    rounds = plan.shape[0]
+    stay_first = jnp.int32(1)
+    for step in range(rounds):
+        odd = step % 2
+        position = lax.rem(device[0] + odd, count)
+        upper = lax.rem(position + 1, count)
+        second = 2 * position + 1
+        second_up = jnp.where((plan[step, 2 * upper] == second) | (plan[step, 2 * upper + 1] == second), 1, 0)
+        send_second = second_up if odd else 1 - second_up
+        flags[step, 0] = stay_first
+        flags[step, 1] = jnp.where(send_second == stay_first, 0, 1)
+        target = device[0] if odd else upper
+        below = lax.rem(target + count - 1, count)
+        from_below = jnp.where(plan[step, 2 * target] // 2 == below, 1, 0)
+        stay_first = 1 - from_below if odd else from_below
+    flags[rounds, 0] = 1 - stay_first
+    flags[rounds, 1] = stay_first
+
+
+def make_flags(plan, device, count):
+    return pl.pallas_call(
+        functools.partial(flags_kernel, count),
+        in_specs=[SMEM, SMEM],
+        out_specs=SMEM,
+        out_shape=jax.ShapeDtypeStruct((plan.shape[0] + 1, 2), jnp.int32),
+        compiler_params=PARAMS,
+        cost_estimate=COST,
+        name="flags",
+    )(plan, device)
+
+
+def first_gram_kernel(snapshots, total, norm, stay, move):
+    rows, width = stay.shape
+    total[...] = jnp.zeros_like(total)
+    norm[...] = jnp.zeros_like(norm)
+
+    def body(one, two, stay_part, move_part):
+        kept, came = one[...], two[...]
+        stay_part[...] = kept
+        move_part[...] = came
+        turned = kept.T
+        total[:width, :] += dot3(split(turned), split(came))
+        total[width:, :] += jnp.sum((came * came).reshape(-1, 8, width), axis=0)
+        norm[...] += jnp.broadcast_to(jnp.sum(turned * turned, axis=1, keepdims=True), norm.shape)
+
+    block = (BLOCK, width)
+    by_row = pl.BlockSpec(block, lambda i: (i, 0))
+    pltpu.emit_pipeline(
+        body,
+        grid=(rows // BLOCK,),
+        in_specs=[by_row, pl.BlockSpec(block, lambda i: (i, 1))],
+        out_specs=[by_row, by_row],
+    )(snapshots, snapshots, stay, move)
 
 
 def first_gram(snapshots, width):
     rows = snapshots.shape[0]
+    vmem = pl.BlockSpec(memory_space=pltpu.VMEM)
+    anywhere = pl.BlockSpec(memory_space=pl.ANY)
     return pl.pallas_call(
         first_gram_kernel,
-        grid=(rows // BLOCK,),
-        in_specs=[pl.BlockSpec((BLOCK, width), lambda i: (i, 0)), pl.BlockSpec((BLOCK, width), lambda i: (i, 1))],
-        out_specs=[whole((width + 8, width)), whole((width, 128))],
+        in_specs=[pl.BlockSpec(memory_space=pltpu.HBM)],
+        out_specs=[vmem, vmem, anywhere, anywhere],
         out_shape=[
             jax.ShapeDtypeStruct((width + 8, width), jnp.float32),
             jax.ShapeDtypeStruct((width, 128), jnp.float32),
+            jax.ShapeDtypeStruct((rows, width), jnp.float32),
+            jax.ShapeDtypeStruct((rows, width), jnp.float32),
         ],
         compiler_params=PARAMS,
+        cost_estimate=COST,
         name="first_gram",
-    )(snapshots, snapshots)
+    )(snapshots)
 
 
 def gram_kernel(turned, came, before, total):
@@ -101,19 +146,19 @@
         body,
         out_shape=jax.ShapeDtypeStruct((width + 8, width), jnp.float32),
         compiler_params=PARAMS,
-        cost_estimate=cost(6 * rows * width * width, 4 * (2 * rows * width + 2 * width * width)),
+        cost_estimate=COST,
         name="gram",
     )(*args)
 
 
-def rotation_kernel(flags, mine, other, norm, stay, move, high, low, sent):
+def rotation_kernel(step, flags, mine, other, norm, stay, move, high, low, sent):
     width = stay.shape[1]
     total = mine[...] + other[...]
     norm_move = jnp.sum(total[width:, :], axis=0, keepdims=True)
     coupled = total[:width, :] / (norm[:, :1] + norm_move + EPSILON)
     turned = coupled.T
-    stay_first = flags[0] == 1
-    send_is_stay = flags[1] == 1
+    stay_first = flags[step, 0] == 1
+    send_is_stay = flags[step, 1] == 1
     coupling = jnp.where(stay_first, coupled, turned)
     coupling_turned = jnp.where(stay_first, turned, coupled)
     identity = eye(width)
@@ -155,15 +200,15 @@
 def view(source, block, grid_of_one):
     array, row, column = source
     if grid_of_one:
-        return pl.BlockSpec(block, lambda *_: (row, column))
+        return pl.BlockSpec(block, lambda *_: (row * BLOCK // block[0], column))
     return pl.BlockSpec(block, lambda i, *_: (row + i, column))
 
 
-def rotation(flags, mine, other, norm, stay, move, blocks):
+def rotation(step, flags, mine, other, norm, stay, move, blocks):
     width = mine.shape[1]
     size = (blocks * BLOCK, width)
     return pl.pallas_call(
-        rotation_kernel,
+        functools.partial(rotation_kernel, step),
         grid=(1,),
         in_specs=[SMEM, whole(mine.shape), whole(other.shape), whole(norm.shape), view(stay, size, True), view(move, size, True)],
         out_specs=[whole((2 * width, 2 * width)), whole((2 * width, 2 * width)), whole(size)],
@@ -173,6 +218,7 @@
             jax.ShapeDtypeStruct(size, jnp.float32),
         ],
         compiler_params=PARAMS,
+        cost_estimate=COST,
         name="rotation",
     )(flags, mine, other, norm, stay[0], move[0])
 
@@ -223,7 +269,7 @@
         out_shape=[piece] * with_sent
         + [piece, jax.ShapeDtypeStruct((width, rows), jnp.float32), jax.ShapeDtypeStruct((width, 128), jnp.float32)],
         compiler_params=PARAMS,
-        cost_estimate=cost(24 * rows * width * width, 20 * rows * width),
+        cost_estimate=COST,
         name="apply",
     )(stay[0], move[0], high, low, *([] if first else [before]))
 
@@ -245,7 +291,7 @@
     width = high.shape[0] // 2
     block = (BLOCK, width)
     first = before is None
-    out = pl.BlockSpec(block, lambda i, place: (start + i, place[0]))
+    out = pl.BlockSpec(block, lambda i, place: (start + i, place[place.shape[0] - 1, 0]))
     by_row = pl.BlockSpec(block, lambda i, place: (i, 0))
     rows = blocks * BLOCK
     return pl.pallas_call(
@@ -261,7 +307,7 @@
         + [jax.ShapeDtypeStruct(shape, jnp.float32)],
         input_output_aliases={} if first else {5: 1 if with_sent else 0},
         compiler_params=PARAMS,
-        cost_estimate=cost(24 * rows * width * width, 20 * rows * width),
+        cost_estimate=COST,
         name="last_apply",
     )(place, stay[0], move[0], high, low, *([] if first else [before]))
 
@@ -279,12 +325,12 @@
             num_scalar_prefetch=1,
             grid=(rows // BLOCK,),
             in_specs=[pl.BlockSpec(block, lambda i, place: (i, 0)), pl.BlockSpec(memory_space=pl.ANY)],
-            out_specs=pl.BlockSpec(block, lambda i, place: (start + i, place[0])),
+            out_specs=pl.BlockSpec(block, lambda i, place: (start + i, place[place.shape[0] - 1, 1])),
         ),
         out_shape=jax.ShapeDtypeStruct(before.shape, jnp.float32),
         input_output_aliases={2: 0},
         compiler_params=PARAMS,
-        cost_estimate=cost(0, 8 * rows * width),
+        cost_estimate=COST,
         name="put",
     )(place, came, before)
 
@@ -298,52 +344,36 @@
     starts = [sum(sizes[:i]) for i in range(len(sizes))]
     device = lax.axis_index("pair")
     count = lax.axis_size("pair")
-    stay = [(snapshots, start, 0) for start in starts]
-    move = [(snapshots, start, 1) for start in starts]
-    stay_first = jnp.bool_(True)
+    total, norm, stay, move = first_gram(snapshots, width)
+    stay = [(stay, start, 0) for start in starts]
+    move = [(move, start, 0) for start in starts]
+    flags = make_flags(plan, device[None], count)
     for round_index in range(rounds):
         last = round_index == rounds - 1
         odd = round_index % 2
-        position = (device + odd) % count
-        upper = (position + 1) % count
-        layout = plan[round_index]
-        upper_zero = lax.dynamic_index_in_dim(layout, 2 * upper, 0, False)
-        upper_one = lax.dynamic_index_in_dim(layout, 2 * upper + 1, 0, False)
-        second_goes_up = (upper_zero == 2 * position + 1) | (upper_one == 2 * position + 1)
-        send_is_second = second_goes_up if odd else ~second_goes_up
-        send_is_stay = send_is_second != stay_first
-        flags = jnp.stack((stay_first, send_is_stay)).astype(jnp.int32)
-        target = device if odd else (device + 1) % count
-        below = (target + count - 1) % count
-        source_zero = lax.dynamic_index_in_dim(layout, 2 * target, 0, False)
-        zero_from_below = source_zero // 2 == below
-        stay_first = ~zero_from_below if odd else zero_from_below
-
         if round_index == 0:
-            total, norm = first_gram(snapshots, width)
             norm = norm + shift(norm, "row", 1)
         else:
             total = None
             for one, two in zip(turned, move):
                 total = gram(one, two[0], total)
         other = shift(total, "row", 1)
-        high, low, outgoing = rotation(flags, total, other, norm, stay[0], move[0], sizes[0])
+        high, low, outgoing = rotation(round_index, flags, total, other, norm, stay[0], move[0], sizes[0])
 
         direction = 2 if odd else -2
         arriving = [shift(outgoing, "pair", direction)]
         if last and rounds % 2 == 0:
-            stay_column = jnp.where(stay_first, 0, 1).astype(jnp.int32)[None]
             field = None
             for piece in range(1, len(sizes)):
                 outgoing, field = last_apply(
-                    stay_column, stay[piece], move[piece], high, low, field, starts[piece], sizes[piece], snapshots.shape, True
+                    flags, stay[piece], move[piece], high, low, field, starts[piece], sizes[piece], snapshots.shape, True
                 )
                 arriving.append(shift(outgoing, "pair", direction))
             (field,) = last_apply(
-                stay_column, stay[0], move[0], high, low, field, starts[0], sizes[0], snapshots.shape, False
+                flags, stay[0], move[0], high, low, field, starts[0], sizes[0], snapshots.shape, False
             )
             for piece, start in zip(arriving, starts):
-                field = put(1 - stay_column, piece, field, start)
+                field = put(flags, piece, field, start)
             return field
         norm = None
         held = [None] * len(sizes)
@@ -357,7 +387,7 @@
         norm = norm + shift(norm, "row", 1)
     stay = shift(jnp.concatenate([value for value, _, _ in stay], axis=0), "pair", 1)
     move = shift(jnp.concatenate([value for value, _, _ in move], axis=0), "pair", 1)
-    stay_first = shift(stay_first.astype(jnp.int32), "pair", 1) == 1
+    stay_first = shift(flags[rounds, 1], "pair", 1) == 1
     return jnp.concatenate(
         (jnp.where(stay_first, stay, move), jnp.where(stay_first, move, stay)), axis=1
     )

time: 259 us -> 235 us (0.907)
  between operations: 16.5 us -> 0.35 us
  local copies, waits for them, and re-layouts: 13.2 us -> 5.09 us
  Pallas kernels: 54.3 us -> 60.4 us
  waiting for transfers between devices: 150 us -> 144 us
    unnamed x38 -> x8, local copies, waits for them, and re-layouts: 11.8 us -> 5.09 us
    ppermute x24, waiting for transfers between devices: 150 us -> 144 us  [shift(): lax.ppermute(value, axis, [(i, (i + by) % size) for i in range(size)])]
    pallas_call x5 -> x6, Pallas kernels: 20 us -> 23.1 us  [the longest x4 18.1 us: rotation(): pl.pallas_call(functools.partial(rotation_kernel, step), grid=(1,), in_sp...]
  transfers between devices with their start and end apart: 24 -> 24, of which waited for: 8 -> 18; matrix products, arithmetic and copies ran while one was open for 1% -> 0% of each run, Pallas kernels for 9% -> 15%
where the time goes in v1:
time: 235 us
  waiting for transfers between devices  144 us (61%)
  Pallas kernels  60.4 us (26%)
  starting transfers between devices  24.4 us (10%)
  local copies, waits for them, and re-layouts  5.09 us (2%)
    ppermute x24, waiting for transfers between devices, shift(): lax.ppermute(value, axis, [(i, (i + by) % size) for i in range(size)])  144 us
    ppermute x24, starting transfers between devices, shift(): lax.ppermute(value, axis, [(i, (i + by) % size) for i in range(size)])  24.4 us
    pallas_call x4, Pallas kernels, rotation(): pl.pallas_call(functools.partial(rotation_kernel, step), grid=(1,), in_sp...  18.1 us
    pallas_call x12, Pallas kernels, apply(): pl.pallas_call(functools.partial(apply_kernel, first, with_sent), grid=(b...  17.3 us
    pallas_call x4, Pallas kernels, last_apply(): pl.pallas_call(functools.partial(last_apply_kernel, first, with_sent), gr...  9.67 us
    pallas_call x4, Pallas kernels, put(): pl.pallas_call(place_kernel, grid_spec=pltpu.PrefetchScalarGridSpec(num_s...  5.72 us
    unnamed x8, local copies, waits for them, and re-layouts  5.09 us
  transfers between devices with their start and end apart: 24, of which 18 were waited for; matrix products, arithmetic and copies ran while one was open for 0% of the time, Pallas kernels for 15%

profile of v1, /device:TPU:0, one launch (start us, length us, event | category | flops | bytes accessed | tf_op | source)
XLA Modules:
  0.0 234.7 jit_solution(2196381204513599030)
XLA Ops:
  0.0 2.2 copy-done.2
  2.2 3.7 %first_gram.1 = (f32[264,256]{1,0:T(8,128)S(1)}, f32[256,128]{1,0:T(8,128)S(1)}, f32[2048,256]{1,0:T(8,128)S(1)}, f32[2048,256]{1,0:T(8,128)S(1)}) custom-call(f32[2048,512]{1,0:T(8,128)S(1)} %copy-done.2), custom_call_target="tpu_custom_call" | custom-call | flops 1024 | bytes 1024 | tf_op jit(solution)/shard_map/first_gram/pallas_call | solution.py:112
  5.9 1.3 copy-done
  7.7 1.3 flags.1.place
  9.1 1.6 copy-done.1
  10.7 4.5 %rotation.4 = (bf16[512,512]{1,0:T(8,128)(2,1)S(1)}, bf16[512,512]{1,0:T(8,128)(2,1)S(1)}, f32[512,256]{1,0:T(8,128)S(1)}) custom-call(s32[5,2]{1,0:T(8,128)S(1)} %flags.1.place, f32[264,256]{1,0:T(8,128)S(1)} %get-tuple-element.74.mine, f32[264,256]{1,0:T(8,128)S(1)} %collective-permute-done.other, f32[256,128]{1,0:T(8,128)S(1)} %add.12.norm, ...), custom_call_target="tpu_custom_call" | custom-call | flops 1024 | bytes 1024 | tf_op jit(solution)/shard_map/rotation/pallas_call | solution.py:210
  15.2 5.1 %collective-permute-start.5 = (f32[512,256]{1,0:T(8,128)S(1)}, f32[512,256]{1,0:T(8,128)S(1)}, u32[]{:S(2)}, u32[]{:S(2)}) collective-permute-start(f32[512,256]{1,0:T(8,128)S(1)} %get-tuple-element.89), channel_id=1, source_target_pairs={{0,12},{2,14},{4,0},{6,2},{8,4},{10,6},{12,8},{14,10},{1,13},{3,15... | collective-permute-start | bytes 1572872 | tf_op jit(solution)/shard_map/ppermute | solution.py:19
  20.3 1.6 apply.12
  22.4 1.5 apply.13
  24.4 1.5 apply.14
  27.2 5.4 %collective-permute-done.5.b.move = f32[512,256]{1,0:T(8,128)S(1)} collective-permute-done((f32[512,256]{1,0:T(8,128)S(1)}, f32[512,256]{1,0:T(8,128)S(1)}, u32[]{:S(2)}, u32[]{:S(2)}) %collective-permute-start.5) | collective-permute-done | bytes 524320 | tf_op jit(solution)/shard_map/ppermute | solution.py:19
  33.0 10.8 %collective-permute-done.4.came.move = f32[512,256]{1,0:T(8,128)S(1)} collective-permute-done((f32[512,256]{1,0:T(8,128)S(1)}, f32[512,256]{1,0:T(8,128)S(1)}, u32[]{:S(2)}, u32[]{:S(2)}) %collective-permute-start.4) | collective-permute-done | bytes 524320 | tf_op jit(solution)/shard_map/ppermute | solution.py:19
  44.2 10.8 %collective-permute-done.3.came.move = f32[512,256]{1,0:T(8,128)S(1)} collective-permute-done((f32[512,256]{1,0:T(8,128)S(1)}, f32[512,256]{1,0:T(8,128)S(1)}, u32[]{:S(2)}, u32[]{:S(2)}) %collective-permute-start.3) | collective-permute-done | bytes 524320 | tf_op jit(solution)/shard_map/ppermute | solution.py:19
  55.5 9.9 %collective-permute-done.2.came.move = f32[512,256]{1,0:T(8,128)S(1)} collective-permute-done((f32[512,256]{1,0:T(8,128)S(1)}, f32[512,256]{1,0:T(8,128)S(1)}, u32[]{:S(2)}, u32[]{:S(2)}) %collective-permute-start.2) | collective-permute-done | bytes 524320 | tf_op jit(solution)/shard_map/ppermute | solution.py:19
  67.6 4.5 %rotation.5 = (bf16[512,512]{1,0:T(8,128)(2,1)S(1)}, bf16[512,512]{1,0:T(8,128)(2,1)S(1)}, f32[512,256]{1,0:T(8,128)S(1)}) custom-call(s32[5,2]{1,0:T(8,128)S(1)} %flags.1.place, f32[264,256]{1,0:T(8,128)S(1)} %gram.15.mine, f32[264,256]{1,0:T(8,128)S(1)} %collective-permute-done.6.other, f32[256,128]{1,0:T(8,128)S(1)} %add.13.norm, ...), custom_call_target="tpu_custom_call" | custom-call | flops 1024 | bytes 1024 | tf_op jit(solution)/shard_map/rotation/pallas_call | solution.py:210
  72.7 1.5 apply.16
  74.2 1.6 collective-permute-start.10
  75.8 1.6 apply.17
  77.4 3.4 %collective-permute-start.9 = (f32[512,256]{1,0:T(8,128)S(1)}, f32[512,256]{1,0:T(8,128)S(1)}, u32[]{:S(2)}, u32[]{:S(2)}) collective-permute-start(f32[512,256]{1,0:T(8,128)S(1)} %get-tuple-element.102), channel_id=1, source_target_pairs={{0,4},{2,6},{4,8},{6,10},{8,12},{10,14},{12,0},{14,2},{1,5},{3,7},... | collective-permute-start | bytes 1572872 | tf_op jit(solution)/shard_map/ppermute | solution.py:19
  80.8 1.6 apply.18
  83.8 5.4 %collective-permute-done.11.b.move = f32[512,256]{1,0:T(8,128)S(1)} collective-permute-done((f32[512,256]{1,0:T(8,128)S(1)}, f32[512,256]{1,0:T(8,128)S(1)}, u32[]{:S(2)}, u32[]{:S(2)}) %collective-permute-start.11) | collective-permute-done | bytes 524320 | tf_op jit(solution)/shard_map/ppermute | solution.py:19
  89.6 10.8 %collective-permute-done.10.came.move = f32[512,256]{1,0:T(8,128)S(1)} collective-permute-done((f32[512,256]{1,0:T(8,128)S(1)}, f32[512,256]{1,0:T(8,128)S(1)}, u32[]{:S(2)}, u32[]{:S(2)}) %collective-permute-start.10) | collective-permute-done | bytes 524320 | tf_op jit(solution)/shard_map/ppermute | solution.py:19
  100.9 10.8 %collective-permute-done.9.came.move = f32[512,256]{1,0:T(8,128)S(1)} collective-permute-done((f32[512,256]{1,0:T(8,128)S(1)}, f32[512,256]{1,0:T(8,128)S(1)}, u32[]{:S(2)}, u32[]{:S(2)}) %collective-permute-start.9) | collective-permute-done | bytes 524320 | tf_op jit(solution)/shard_map/ppermute | solution.py:19
  112.1 10.4 %collective-permute-done.8.came.move = f32[512,256]{1,0:T(8,128)S(1)} collective-permute-done((f32[512,256]{1,0:T(8,128)S(1)}, f32[512,256]{1,0:T(8,128)S(1)}, u32[]{:S(2)}, u32[]{:S(2)}) %collective-permute-start.8) | collective-permute-done | bytes 524320 | tf_op jit(solution)/shard_map/ppermute | solution.py:19
  123.4 1.2 collective-permute-done.13
  124.7 4.5 %rotation.6 = (bf16[512,512]{1,0:T(8,128)(2,1)S(1)}, bf16[512,512]{1,0:T(8,128)(2,1)S(1)}, f32[512,256]{1,0:T(8,128)S(1)}) custom-call(s32[5,2]{1,0:T(8,128)S(1)} %flags.1.place, f32[264,256]{1,0:T(8,128)S(1)} %gram.19.mine, f32[264,256]{1,0:T(8,128)S(1)} %collective-permute-done.12.other, f32[256,128]{1,0:T(8,128)S(1)} %add.14.norm, ...), custom_call_target="tpu_custom_call" | custom-call | flops 1024 | bytes 1024 | tf_op jit(solution)/shard_map/rotation/pallas_call | solution.py:210
  129.2 1.8 collective-permute-start.17
  131.0 1.5 apply.20
  132.7 1.5 apply.21
  134.3 1.6 apply.22
  135.8 3.2 %collective-permute-start.14 = (f32[512,256]{1,0:T(8,128)S(1)}, f32[512,256]{1,0:T(8,128)S(1)}, u32[]{:S(2)}, u32[]{:S(2)}) collective-permute-start(f32[512,256]{1,0:T(8,128)S(1)} %get-tuple-element.117), channel_id=1, source_target_pairs={{0,12},{2,14},{4,0},{6,2},{8,4},{10,6},{12,8},{14,10},{1,13},{3,15... | collective-permute-start | bytes 1572872 | tf_op jit(solution)/shard_map/ppermute | solution.py:19
  140.2 3.9 %collective-permute-done.17.b.move = f32[512,256]{1,0:T(8,128)S(1)} collective-permute-done((f32[512,256]{1,0:T(8,128)S(1)}, f32[512,256]{1,0:T(8,128)S(1)}, u32[]{:S(2)}, u32[]{:S(2)}) %collective-permute-start.17) | collective-permute-done | bytes 524320 | tf_op jit(solution)/shard_map/ppermute | solution.py:19
  144.4 10.8 %collective-permute-done.16.came.move = f32[512,256]{1,0:T(8,128)S(1)} collective-permute-done((f32[512,256]{1,0:T(8,128)S(1)}, f32[512,256]{1,0:T(8,128)S(1)}, u32[]{:S(2)}, u32[]{:S(2)}) %collective-permute-start.16) | collective-permute-done | bytes 524320 | tf_op jit(solution)/shard_map/ppermute | solution.py:19
  155.7 10.8 %collective-permute-done.15.came.move = f32[512,256]{1,0:T(8,128)S(1)} collective-permute-done((f32[512,256]{1,0:T(8,128)S(1)}, f32[512,256]{1,0:T(8,128)S(1)}, u32[]{:S(2)}, u32[]{:S(2)}) %collective-permute-start.15) | collective-permute-done | bytes 524320 | tf_op jit(solution)/shard_map/ppermute | solution.py:19
  166.9 10.0 %collective-permute-done.14.came.move = f32[512,256]{1,0:T(8,128)S(1)} collective-permute-done((f32[512,256]{1,0:T(8,128)S(1)}, f32[512,256]{1,0:T(8,128)S(1)}, u32[]{:S(2)}, u32[]{:S(2)}) %collective-permute-start.14) | collective-permute-done | bytes 524320 | tf_op jit(solution)/shard_map/ppermute | solution.py:19
  179.2 4.5 %rotation.7 = (bf16[512,512]{1,0:T(8,128)(2,1)S(1)}, bf16[512,512]{1,0:T(8,128)(2,1)S(1)}, f32[512,256]{1,0:T(8,128)S(1)}) custom-call(s32[5,2]{1,0:T(8,128)S(1)} %flags.1.place, f32[264,256]{1,0:T(8,128)S(1)} %gram.23.mine, f32[264,256]{1,0:T(8,128)S(1)} %collective-permute-done.18.other, f32[256,128]{1,0:T(8,128)S(1)} %add.15.norm, ...), custom_call_target="tpu_custom_call" | custom-call | flops 1024 | bytes 1024 | tf_op jit(solution)/shard_map/rotation/pallas_call | solution.py:210
  183.8 2.5 %last_apply.4 = (f32[512,256]{1,0:T(8,128)S(1)}, f32[2048,512]{1,0:T(8,128)}) custom-call(s32[5,2]{1,0:T(8,128)S(1)} %flags.1.place, f32[512,256]{1,0:T(8,128)S(1)} %get-tuple-element.131.stay, f32[512,256]{1,0:T(8,128)S(1)} %collective-permute-done.16.came.move, bf16[512,512]{1,0:T(8,128)(2,1)S(1)} %get-tuple-element.128.high, ...), custom_call_target="tpu_custom_call" | custom-call | flops 1024 | bytes 1024 | tf_op jit(solution)/shard_map/last_apply/pallas_call | solution.py:297
  186.3 2.5 %last_apply.5 = (f32[512,256]{1,0:T(8,128)S(1)}, f32[2048,512]{1,0:T(8,128)}) custom-call(s32[5,2]{1,0:T(8,128)S(1)} %flags.1.place, f32[512,256]{1,0:T(8,128)S(1)} %get-tuple-element.130.stay, f32[512,256]{1,0:T(8,128)S(1)} %collective-permute-done.15.came.move, bf16[512,512]{1,0:T(8,128)(2,1)S(1)} %get-tuple-element.128.high, ...), custom_call_target="tpu_custom_call", output_to_operand_aliasing={{1}: (5, {})} | custom-call | flops 1024 | bytes 1024 | tf_op jit(solution)/shard_map/last_apply/pallas_call | solution.py:297
  189.9 3.5 %collective-permute-start.22 = (f32[512,256]{1,0:T(8,128)S(1)}, f32[512,256]{1,0:T(8,128)S(1)}, u32[]{:S(2)}, u32[]{:S(2)}) collective-permute-start(f32[512,256]{1,0:T(8,128)S(1)} %get-tuple-element.136), channel_id=1, source_target_pairs={{0,4},{2,6},{4,8},{6,10},{8,12},{10,14},{12,0},{14,2},{1,5},{3,7},... | collective-permute-start | bytes 1572872 | tf_op jit(solution)/shard_map/ppermute | solution.py:19
  193.5 2.5 %last_apply.6 = (f32[512,256]{1,0:T(8,128)S(1)}, f32[2048,512]{1,0:T(8,128)}) custom-call(s32[5,2]{1,0:T(8,128)S(1)} %flags.1.place, f32[512,256]{1,0:T(8,128)S(1)} %get-tuple-element.116.stay, f32[512,256]{1,0:T(8,128)S(1)} %collective-permute-done.14.came.move, bf16[512,512]{1,0:T(8,128)(2,1)S(1)} %get-tuple-element.128.high, ...), custom_call_target="tpu_custom_call", output_to_operand_aliasing={{1}: (5, {})} | custom-call | flops 1024 | bytes 1024 | tf_op jit(solution)/shard_map/last_apply/pallas_call | solution.py:297
  196.3 2.1 last_apply.7.before
  198.4 1.9 collective-permute-done.23.came
  200.3 1.4 put.4.before
  201.8 21.0 %collective-permute-done.22.came = f32[512,256]{1,0:T(8,128)S(1)} collective-permute-done((f32[512,256]{1,0:T(8,128)S(1)}, f32[512,256]{1,0:T(8,128)S(1)}, u32[]{:S(2)}, u32[]{:S(2)}) %collective-permute-start.22) | collective-permute-done | bytes 524320 | tf_op jit(solution)/shard_map/ppermute | solution.py:19
  222.8 1.4 put.5.before
  224.2 1.4 put.6.before
  225.7 7.6 %collective-permute-done.20.came = f32[512,256]{1,0:T(8,128)S(1)} collective-permute-done((f32[512,256]{1,0:T(8,128)S(1)}, f32[512,256]{1,0:T(8,128)S(1)}, u32[]{:S(2)}, u32[]{:S(2)}) %collective-permute-start.20) | collective-permute-done | bytes 524320 | tf_op jit(solution)/shard_map/ppermute | solution.py:19
  233.2 1.4 put.7
  (50 shorter events, 16.4 us)
Async XLA Ops:
  0.0 2.2 copy-start.2
  2.2 5.5 %copy-start.3 = (s32[4,16]{1,0:T(4,128)S(1)}, s32[4,16]{1,0:T(4,128)}, u32[]{:S(2)}) copy-start(s32[4,16]{1,0:T(4,128)} %plan.1) | copy-start | bytes 772
  5.9 1.3 copy-start
  7.2 1.8 collective-permute-start
  7.7 1.4 collective-permute-start.1
  9.1 1.6 copy-start.1
  15.2 17.4 %collective-permute-start.5 = (f32[512,256]{1,0:T(8,128)S(1)}, f32[512,256]{1,0:T(8,128)S(1)}, u32[]{:S(2)}, u32[]{:S(2)}) collective-permute-start(f32[512,256]{1,0:T(8,128)S(1)} %get-tuple-element.89), channel_id=1, source_target_pairs={{0,12},{2,14},{4,0},{6,2},{8,4},{10,6},{12,8},{14,10},{1,13},{3,15... | collective-permute-start | bytes 1572872 | tf_op jit(solution)/shard_map/ppermute | solution.py:19
  21.9 22.0 %collective-permute-start.4 = (f32[512,256]{1,0:T(8,128)S(1)}, f32[512,256]{1,0:T(8,128)S(1)}, u32[]{:S(2)}, u32[]{:S(2)}) collective-permute-start(f32[512,256]{1,0:T(8,128)S(1)} %get-tuple-element.86), channel_id=1, source_target_pairs={{0,12},{2,14},{4,0},{6,2},{8,4},{10,6},{12,8},{14,10},{1,13},{3,15... | collective-permute-start | bytes 1572872 | tf_op jit(solution)/shard_map/ppermute | solution.py:19
  23.9 31.2 %collective-permute-start.3 = (f32[512,256]{1,0:T(8,128)S(1)}, f32[512,256]{1,0:T(8,128)S(1)}, u32[]{:S(2)}, u32[]{:S(2)}) collective-permute-start(f32[512,256]{1,0:T(8,128)S(1)} %get-tuple-element.84), channel_id=1, source_target_pairs={{0,12},{2,14},{4,0},{6,2},{8,4},{10,6},{12,8},{14,10},{1,13},{3,15... | collective-permute-start | bytes 1572872 | tf_op jit(solution)/shard_map/ppermute | solution.py:19
  25.9 39.5 %collective-permute-start.2 = (f32[512,256]{1,0:T(8,128)S(1)}, f32[512,256]{1,0:T(8,128)S(1)}, u32[]{:S(2)}, u32[]{:S(2)}) collective-permute-start(f32[512,256]{1,0:T(8,128)S(1)} %get-tuple-element.81), channel_id=1, source_target_pairs={{0,12},{2,14},{4,0},{6,2},{8,4},{10,6},{12,8},{14,10},{1,13},{3,15... | collective-permute-start | bytes 1572872 | tf_op jit(solution)/shard_map/ppermute | solution.py:19
  65.8 1.8 collective-permute-start.6
  65.9 1.7 collective-permute-start.7
  72.2 17.0 %collective-permute-start.11 = (f32[512,256]{1,0:T(8,128)S(1)}, f32[512,256]{1,0:T(8,128)S(1)}, u32[]{:S(2)}, u32[]{:S(2)}) collective-permute-start(f32[512,256]{1,0:T(8,128)S(1)} %get-tuple-element.107), channel_id=1, source_target_pairs={{0,4},{2,6},{4,8},{6,10},{8,12},{10,14},{12,0},{14,2},{1,5},{3,7},... | collective-permute-start | bytes 1572872 | tf_op jit(solution)/shard_map/ppermute | solution.py:19
  74.2 26.2 %collective-permute-start.10 = (f32[512,256]{1,0:T(8,128)S(1)}, f32[512,256]{1,0:T(8,128)S(1)}, u32[]{:S(2)}, u32[]{:S(2)}) collective-permute-start(f32[512,256]{1,0:T(8,128)S(1)} %get-tuple-element.104), channel_id=1, source_target_pairs={{0,4},{2,6},{4,8},{6,10},{8,12},{10,14},{12,0},{14,2},{1,5},{3,7},... | collective-permute-start | bytes 1572872 | tf_op jit(solution)/shard_map/ppermute | solution.py:19
  77.4 34.3 %collective-permute-start.9 = (f32[512,256]{1,0:T(8,128)S(1)}, f32[512,256]{1,0:T(8,128)S(1)}, u32[]{:S(2)}, u32[]{:S(2)}) collective-permute-start(f32[512,256]{1,0:T(8,128)S(1)} %get-tuple-element.102), channel_id=1, source_target_pairs={{0,4},{2,6},{4,8},{6,10},{8,12},{10,14},{12,0},{14,2},{1,5},{3,7},... | collective-permute-start | bytes 1572872 | tf_op jit(solution)/shard_map/ppermute | solution.py:19
  82.4 40.0 %collective-permute-start.8 = (f32[512,256]{1,0:T(8,128)S(1)}, f32[512,256]{1,0:T(8,128)S(1)}, u32[]{:S(2)}, u32[]{:S(2)}) collective-permute-start(f32[512,256]{1,0:T(8,128)S(1)} %get-tuple-element.99), channel_id=1, source_target_pairs={{0,4},{2,6},{4,8},{6,10},{8,12},{10,14},{12,0},{14,2},{1,5},{3,7},... | collective-permute-start | bytes 1572872 | tf_op jit(solution)/shard_map/ppermute | solution.py:19
  122.9 1.8 collective-permute-start.12
  122.9 1.7 collective-permute-start.13
  129.2 14.8 %collective-permute-start.17 = (f32[512,256]{1,0:T(8,128)S(1)}, f32[512,256]{1,0:T(8,128)S(1)}, u32[]{:S(2)}, u32[]{:S(2)}) collective-permute-start(f32[512,256]{1,0:T(8,128)S(1)} %get-tuple-element.125), channel_id=1, source_target_pairs={{0,12},{2,14},{4,0},{6,2},{8,4},{10,6},{12,8},{14,10},{1,13},{3,15... | collective-permute-start | bytes 1572872 | tf_op jit(solution)/shard_map/ppermute | solution.py:19
  132.6 22.7 %collective-permute-start.16 = (f32[512,256]{1,0:T(8,128)S(1)}, f32[512,256]{1,0:T(8,128)S(1)}, u32[]{:S(2)}, u32[]{:S(2)}) collective-permute-start(f32[512,256]{1,0:T(8,128)S(1)} %get-tuple-element.122), channel_id=1, source_target_pairs={{0,12},{2,14},{4,0},{6,2},{8,4},{10,6},{12,8},{14,10},{1,13},{3,15... | collective-permute-start | bytes 1572872 | tf_op jit(solution)/shard_map/ppermute | solution.py:19
  134.2 32.3 %collective-permute-start.15 = (f32[512,256]{1,0:T(8,128)S(1)}, f32[512,256]{1,0:T(8,128)S(1)}, u32[]{:S(2)}, u32[]{:S(2)}) collective-permute-start(f32[512,256]{1,0:T(8,128)S(1)} %get-tuple-element.120), channel_id=1, source_target_pairs={{0,12},{2,14},{4,0},{6,2},{8,4},{10,6},{12,8},{14,10},{1,13},{3,15... | collective-permute-start | bytes 1572872 | tf_op jit(solution)/shard_map/ppermute | solution.py:19
  135.8 41.1 %collective-permute-start.14 = (f32[512,256]{1,0:T(8,128)S(1)}, f32[512,256]{1,0:T(8,128)S(1)}, u32[]{:S(2)}, u32[]{:S(2)}) collective-permute-start(f32[512,256]{1,0:T(8,128)S(1)} %get-tuple-element.117), channel_id=1, source_target_pairs={{0,12},{2,14},{4,0},{6,2},{8,4},{10,6},{12,8},{14,10},{1,13},{3,15... | collective-permute-start | bytes 1572872 | tf_op jit(solution)/shard_map/ppermute | solution.py:19
  177.3 1.8 collective-permute-start.18
  177.4 1.7 collective-permute-start.19
  183.7 16.6 %collective-permute-start.23 = (f32[512,256]{1,0:T(8,128)S(1)}, f32[512,256]{1,0:T(8,128)S(1)}, u32[]{:S(2)}, u32[]{:S(2)}) collective-permute-start(f32[512,256]{1,0:T(8,128)S(1)} %get-tuple-element.137), channel_id=1, source_target_pairs={{0,4},{2,6},{4,8},{6,10},{8,12},{10,14},{12,0},{14,2},{1,5},{3,7},... | collective-permute-start | bytes 1572872 | tf_op jit(solution)/shard_map/ppermute | solution.py:19
  188.8 35.4 %collective-permute-start.21 = (f32[512,256]{1,0:T(8,128)S(1)}, f32[512,256]{1,0:T(8,128)S(1)}, u32[]{:S(2)}, u32[]{:S(2)}) collective-permute-start(f32[512,256]{1,0:T(8,128)S(1)} %get-tuple-element.135), channel_id=1, source_target_pairs={{0,4},{2,6},{4,8},{6,10},{8,12},{10,14},{12,0},{14,2},{1,5},{3,7},... | collective-permute-start | bytes 1572872 | tf_op jit(solution)/shard_map/ppermute | solution.py:19
  189.9 32.9 %collective-permute-start.22 = (f32[512,256]{1,0:T(8,128)S(1)}, f32[512,256]{1,0:T(8,128)S(1)}, u32[]{:S(2)}, u32[]{:S(2)}) collective-permute-start(f32[512,256]{1,0:T(8,128)S(1)} %get-tuple-element.136), channel_id=1, source_target_pairs={{0,4},{2,6},{4,8},{6,10},{8,12},{10,14},{12,0},{14,2},{1,5},{3,7},... | collective-permute-start | bytes 1572872 | tf_op jit(solution)/shard_map/ppermute | solution.py:19
  196.0 37.3 %collective-permute-start.20 = (f32[512,256]{1,0:T(8,128)S(1)}, f32[512,256]{1,0:T(8,128)S(1)}, u32[]{:S(2)}, u32[]{:S(2)}) collective-permute-start(f32[512,256]{1,0:T(8,128)S(1)} %get-tuple-element.134), channel_id=1, source_target_pairs={{0,4},{2,6},{4,8},{6,10},{8,12},{10,14},{12,0},{14,2},{1,5},{3,7},... | collective-permute-start | bytes 1572872 | tf_op jit(solution)/shard_map/ppermute | solution.py:19
